TPU v7x, 32 devices: a whole 2x2x4 slice. The times are simulated.
32 devices in a mesh: groups: 2 (over y), dev: 8 (over z, x), tp: 2 (over core).
Axes of the slice: x: 2, y: 2, z: 4, core: 2. Of those that a mesh axis runs over, the one named last changes fastest.
Arguments:
- residual: bfloat16 [2048, 1024], P(('groups', 'dev'), 'tp'), parts along dimension 0, may hold values from -6 to 6
- queries: bfloat16 [2048, 1024], P(('groups', 'dev'), 'tp'), parts along dimension 0, may hold values from -8 to 8
- keys: bfloat16 [2048, 1024], P(('groups', 'dev'), 'tp'), parts along dimension 0, may hold values from -8 to 8
- values: bfloat16 [2048, 1024], P(('groups', 'dev'), 'tp'), parts along dimension 0, may hold values from -6 to 6
- tile_lists: int32 [64, 3], P(('groups', 'dev')), parts along dimension 0, may hold values from 0 to 3, as said below
- node_counts: int32 [16, 4], P(('groups', 'dev')), parts along dimension 0, may hold values from 1 to 64, 128 in all within a row
- norm_gain: float32 [1024], P('tp'), may hold values from 0.5 to 1.5
- expert_ids: int32 [2048, 2], P(('groups', 'dev')), parts along dimension 0, may hold values from 0 to 3, all different within a row; in each aligned block of 128 rows (0 to 127, 128 to 255, ...) at most 128 rows name the same one
- gate_codes: int32 [2048, 2], P(('groups', 'dev')), parts along dimension 0, may hold values from 8192 to 57344
- up_weight: bfloat16 [8, 1024, 2048], P('dev', None, 'tp'), may hold values from -0.1875 to 0.1875
- down_weight: bfloat16 [8, 2048, 1024], P('dev', 'tp'), may hold values from -0.09375 to 0.09375
Outputs:
- mixed: bfloat16 [2048, 1024], P(('groups', 'dev'), 'tp'), parts along dimension 0
There are 2 independent parts, one for each index of `groups`. A program takes and returns all parts, laid end to end along the dimension named above; an argument that names none is the same for every part. Nothing has to cross between parts.
Inputs may be any that keep to these rules, and one draw needn't show every extreme that they name: `tile_lists`: entry 0 of each row is the tile's own index within its block of 4 tiles; the others are indices of the same or earlier tiles of that block. `expert_ids`: each row names 2 different experts; in the rows of one device no expert is named more than 128 times, and some expert reaches 128.
All inputs are finite; a program needn't handle non-finite values.
Results may differ from a plain program's by a relative error of at most 0.0047.
Values may be sent and summed in bfloat16 or wider, within the bound.
A program may use at most 64 MiB of HBM per device.

v0:
```python
import jax
import jax.numpy as jnp
from jax import lax
from jax.sharding import PartitionSpec as P

D = 1024
HEAD = 64
TOPK = 2


epsilon = 1e-06


def from_partner(value, axis, bit):
    return lax.ppermute(value, axis, [(i, i ^ 1 << bit) for i in range(lax.axis_size(axis))])


def cone_mask(tile_lists, node_counts, node_total):
    tile_count = tile_lists.shape[0]
    tile_size = node_total // tile_count
    tile_ids = jnp.arange(tile_count, dtype=jnp.int32)
    tile_ok = jnp.any(tile_lists[:, :, None] == tile_ids[None, None, :], axis=1)
    node_ok = jnp.broadcast_to(
        tile_ok[:, None, :, None], (tile_count, tile_size, tile_count, tile_size)
    ).reshape(node_total, node_total)
    nodes = jnp.arange(node_total, dtype=jnp.int32)
    graph_ends = jnp.cumsum(node_counts)
    graph_of = jnp.sum((nodes[:, None] >= graph_ends[None, :]).astype(jnp.int32), axis=1)
    same_graph = graph_of[:, None] == graph_of[None, :]
    return node_ok & same_graph & (nodes[None, :] <= nodes[:, None])


def cone_attention(queries, keys, values, allowed):
    node_total, width = queries.shape
    head_count = width // HEAD
    query_heads = queries.reshape(node_total, head_count, HEAD)
    key_heads = keys.reshape(node_total, head_count, HEAD)
    value_heads = values.reshape(node_total, head_count, HEAD)
    scores = jnp.einsum(
        "qhd,khd->hqk", query_heads, key_heads, preferred_element_type=jnp.float32
    ) * HEAD ** (-0.5)
    scores = jnp.where(allowed[None], scores, -1e30)
    highest = jnp.max(scores, axis=2, keepdims=True)
    weights = jnp.where(allowed[None], jnp.exp(scores - highest), 0.0)
    denominator = jnp.sum(weights, axis=2, keepdims=True)
    probs = (weights / denominator).astype(jnp.bfloat16)
    attended = jnp.einsum("hqk,khd->qhd", probs, value_heads, preferred_element_type=jnp.float32)
    return attended.reshape(node_total, width)


def slots_of(flat_ids, expert_count):
    onehot = (flat_ids[..., None] == jnp.arange(expert_count, dtype=jnp.int32)).astype(jnp.int32)
    before = jnp.cumsum(onehot, axis=-2) - onehot
    return jnp.sum(before * onehot, axis=-1)


def per_device(
    residual,
    queries,
    keys,
    values,
    tile_lists,
    node_counts,
    norm_gain,
    expert_ids,
    gate_codes,
    up_weight,
    down_weight,
):
    node_total = residual.shape[0]
    half_width = residual.shape[1]
    quarter = half_width // 2
    devices = lax.axis_size("dev")
    experts = devices // 2
    capacity = 8 * node_total // devices
    parity = lax.axis_index("dev") % 2
    allowed = cone_mask(tile_lists, node_counts[0], node_total)
    stream = residual.astype(jnp.float32) + cone_attention(queries, keys, values, allowed)
    squares = lax.psum(jnp.sum(stream * stream, axis=1), "tp")
    normed = (stream * lax.rsqrt(squares / D + epsilon)[:, None] * norm_gain).astype(jnp.bfloat16)
    flat_ids = expert_ids.reshape(-1)
    slot_index = slots_of(flat_ids, experts)
    row_ids = jnp.arange(experts * capacity, dtype=jnp.int32)
    hits = (flat_ids[None, :] == (row_ids // capacity)[:, None]) & (
        slot_index[None, :] == (row_ids % capacity)[:, None]
    )
    dispatch = jnp.sum(
        hits.reshape(experts * capacity, node_total, TOPK).astype(jnp.int32), axis=2
    ).astype(jnp.bfloat16)
    packed = jnp.dot(dispatch, normed, preferred_element_type=jnp.float32).astype(jnp.bfloat16)
    outgoing = jnp.broadcast_to(
        packed.reshape(experts, 1, capacity, half_width), (experts, 2, capacity, half_width)
    ).reshape(devices * capacity, half_width)
    arrived = lax.all_to_all(outgoing, "dev", split_axis=0, concat_axis=0, tiled=True)
    w_up = up_weight[0]
    w_down = down_weight[0]
    up_whole, down_whole = (
        lax.all_gather(w_up, "tp", axis=1, tiled=True),
        lax.all_gather(w_down, "tp", axis=0, tiled=True),
    )
    served = lax.all_to_all(arrived, "tp", split_axis=0, concat_axis=1, tiled=True)
    hidden = jax.nn.gelu(jnp.dot(served, up_whole, preferred_element_type=jnp.float32)).astype(
        jnp.bfloat16
    )
    served_out = jnp.dot(hidden, down_whole, preferred_element_type=jnp.float32)
    summed_half = lax.all_to_all(served_out, "tp", split_axis=1, concat_axis=0, tiled=True)
    outgoing_share = lax.dynamic_slice_in_dim(summed_half, (1 - parity) * quarter, quarter, 1)
    kept_share = lax.dynamic_slice_in_dim(summed_half, parity * quarter, quarter, 1)
    finished = (
        kept_share
        + from_partner(outgoing_share.astype(jnp.bfloat16), "dev", 0).astype(outgoing_share.dtype)
    ).astype(jnp.bfloat16)
    returned = lax.all_to_all(finished, "dev", split_axis=0, concat_axis=1, tiled=True)
    returned = returned.reshape(capacity * experts, half_width)
    node_slots = slot_index.reshape(node_total, TOPK)
    gates = gate_codes.astype(jnp.float32) / 65536.0
    back_rows = jnp.arange(capacity * experts, dtype=jnp.int32)
    added = jnp.zeros((node_total, half_width), jnp.float32)
    for which in range(TOPK):
        picker = (
            (expert_ids[:, which][None, :] == (back_rows % experts)[:, None])
            & (node_slots[:, which][None, :] == (back_rows // experts)[:, None])
        ).astype(jnp.bfloat16)
        fetched = lax.dot_general(
            picker, returned, (((0,), (0,)), ((), ())), preferred_element_type=jnp.float32
        )
        added = added + gates[:, which : which + 1] * fetched
    return (stream + added).astype(jnp.bfloat16)


def solution(mesh):
    in_specs = (
        P(("groups", "dev"), "tp"),
        P(("groups", "dev"), "tp"),
        P(("groups", "dev"), "tp"),
        P(("groups", "dev"), "tp"),
        P(("groups", "dev"), None),
        P(("groups", "dev"), None),
        P("tp"),
        P(("groups", "dev"), None),
        P(("groups", "dev"), None),
        P("dev", None, "tp"),
        P("dev", "tp", None),
    )
    out_specs = P(("groups", "dev"), "tp")
    return jax.shard_map(
        per_device, mesh=mesh, in_specs=in_specs, out_specs=out_specs, check_vma=False
    )
```

profile of v0, /device:TPU:0, one launch (start us, length us, event | category | flops | bytes accessed | tf_op | source)
XLA Modules:
  0.0 112.6 jit_solution(8624290696425841368)
XLA Ops:
  6.6 0.7 all-gather.5.cloned.1.call-update
  7.4 0.7 all-gather.7.cloned.1.call-update
  8.1 0.1 copy.66
  8.2 0.1 eq.163
  8.3 0.1 eq.159
  8.5 0.1 copy.59
  8.6 0.1 fusion.43
  8.7 0.1 copy.60
  8.8 0.1 broadcast_in_dim.24
  8.9 0.1 reshape.200
  9.0 0.2 reduce-window.18
  9.2 1.2 %reduce-window.19 = s32[4,2,128]{2,1,0:T(2,128)S(1)} reduce-window(s32[4,2,128]{2,1,0:T(2,128)S(1)} %compare_convert_fusion, s32[]{:T(128)} %constant.90.clone.1), window={size=1x1x128 pad=0_0x0_0x127_0}, to_apply=%region_5.6 | reduce-window | flops 130048 | bytes 8196 | tf_op jit(solution)/shard_map/reduce-window.1
  10.4 0.1 slice.32
  10.5 0.1 copy.68
  10.7 0.1 copy.69
  10.8 0.1 reshape.208
  11.1 0.1 copy.61
  11.2 0.1 copy.62
  11.4 0.1 copy.63
  11.5 0.1 convert_reduce_fusion.1
  11.6 0.1 fusion.42
  11.7 0.4 fusion.62
  12.1 0.3 fusion.18
  12.3 0.3 fusion.24
  12.6 0.1 copy.65
  12.8 0.1 multiply_reduce_fusion
  12.9 2.6 %psum.7 = f32[128]{0:T(128)S(1)} all-reduce(f32[128]{0:T(128)S(1)} %multiply_reduce_fusion), channel_id=1, replica_groups=mesh['groups'=2,'dev'=8,'tp'=2] {'tp'}, use_global_device_ids=true, to_apply=%region_10.11 | all-reduce | flops 128 | bytes 1024 | tf_op jit(solution)/shard_map/psum | solution.py:79
  15.5 0.2 convert_reduce_fusion
  15.7 0.4 convolution_convert_fusion
  16.1 1.2 %broadcast_in_dim.29 = bf16[4,2,128,512]{3,2,1,0:T(8,128)(2,1)} broadcast(bf16[4,128,512]{2,1,0:T(8,128)(2,1)S(1)} %bitcast.75), dimensions={0,2,3} | broadcast | bytes 1572864 | tf_op jit(solution)/shard_map/broadcast_in_dim | solution.py:91
  17.3 7.1 %all-to-all-start = ((bf16[8,128,512]{2,1,0:T(8,128)(2,1)}), bf16[8,128,512]{2,1,0:T(8,128)(2,1)S(1)}, u32[]{:S(2)}, u32[]{:S(2)}) async-start(bf16[8,128,512]{2,1,0:T(8,128)(2,1)} %bitcast.12), calls=%async_computation | async-start | bytes 2097152 | tf_op jit(solution)/shard_map/all_to_all | solution.py:94
  24.4 26.1 %all-to-all-done = bf16[8,128,512]{2,1,0:T(8,128)(2,1)S(1)} async-done(((bf16[8,128,512]{2,1,0:T(8,128)(2,1)}), bf16[8,128,512]{2,1,0:T(8,128)(2,1)S(1)}, u32[]{:S(2)}, u32[]{:S(2)}) %all-to-all-start) | async-done | bytes 1048608 | tf_op jit(solution)/shard_map/all_to_all | solution.py:94
  50.5 4.6 %all_to_all.63 = bf16[2,512,512]{2,1,0:T(8,128)(2,1)S(1)} all-to-all(bf16[2,512,512]{2,1,0:T(8,128)(2,1)S(1)} %bitcast.73), channel_id=1, replica_groups=mesh['groups'=2,'dev'=8,'tp'=2] {'tp'}, dimensions={0} | all-to-all | bytes 2097152 | tf_op jit(solution)/shard_map/all_to_all | solution.py:101
  55.1 0.5 copy.71
  55.7 8.5 %fusion.9 = f32[512,1024]{1,0:T(8,128)S(1)} fusion(bf16[1,2048,1024]{2,1,0:T(8,128)(2,1)} %all-gather.7.cloned.1.call-done, bf16[512,1024]{0,1:T(8,128)(2,1)S(1)} %bitcast.78, bf16[1,1024,2048]{2,1,0:T(8,128)(2,1)} %all-gather.5.cloned.1.call-done), kind=kOutput, calls=%fused_computation.10 | convolution fusion | flops 4304404480 | bytes 11534336 | tf_op jit(solution)/shard_map/dot_general | solution.py:105
  64.2 0.2 copy.79
  64.4 5.5 %all_to_all.64 = f32[512,2,512]{2,0,1:T(8,128)S(1)} all-to-all(f32[512,2,512]{2,0,1:T(8,128)S(1)} %bitcast.70), channel_id=1, replica_groups=mesh['groups'=2,'dev'=8,'tp'=2] {'tp'}, dimensions={1} | all-to-all | bytes 4194304 | tf_op jit(solution)/shard_map/all_to_all | solution.py:106
  70.0 0.9 dynamic-slice_convert_fusion
  70.8 1.4 %collective-permute-start = (bf16[1024,256]{1,0:T(8,128)(2,1)}, bf16[1024,256]{1,0:T(8,128)(2,1)S(1)}, u32[]{:S(2)}, u32[]{:S(2)}) collective-permute-start(bf16[1024,256]{1,0:T(8,128)(2,1)} %dynamic-slice_convert_fusion), channel_id=1, source_target_pairs={{0,2},{2,0},{4,6},{6,4},{8,10},{10,8},{12,14},{14,12},{1,3},{3,1},... | collective-permute-start | bytes 1572872 | tf_op jit(solution)/shard_map/ppermute | solution.py:15
  72.2 12.7 %collective-permute-done = bf16[1024,256]{1,0:T(8,128)(2,1)S(1)} collective-permute-done((bf16[1024,256]{1,0:T(8,128)(2,1)}, bf16[1024,256]{1,0:T(8,128)(2,1)S(1)}, u32[]{:S(2)}, u32[]{:S(2)}) %collective-permute-start) | collective-permute-done | bytes 524320 | tf_op jit(solution)/shard_map/ppermute | solution.py:15
  85.0 1.0 add_convert_fusion
  86.0 3.6 %all-to-all-start.3 = ((bf16[8,128,256]{2,1,0:T(8,128)(2,1)}), bf16[8,128,256]{2,1,0:T(8,128)(2,1)S(1)}, u32[]{:S(2)}, u32[]{:S(2)}) async-start(bf16[8,128,256]{2,1,0:T(8,128)(2,1)} %bitcast.21), calls=%async_computation.3 | async-start | bytes 1048576 | tf_op jit(solution)/shard_map/all_to_all | solution.py:113
  89.6 0.2 slice_reduce_fusion
  89.9 13.8 %all-to-all-done.3 = bf16[8,128,256]{2,1,0:T(8,128)(2,1)S(1)} async-done(((bf16[8,128,256]{2,1,0:T(8,128)(2,1)}), bf16[8,128,256]{2,1,0:T(8,128)(2,1)S(1)}, u32[]{:S(2)}, u32[]{:S(2)}) %all-to-all-start.3) | async-done | bytes 524320 | tf_op jit(solution)/shard_map/all_to_all | solution.py:113
  103.7 0.3 copy.73
  104.0 0.2 reshape.209
  104.2 0.5 convolution_multiply_fusion.2
  104.6 1.1 fusion.21
  (38 shorter events, 0.4 us)
Async XLA Ops:
  6.5 1.5 %copy-start.6 = (s32[128,2]{0,1:T(2,128)S(1)}, s32[128,2]{0,1:T(2,128)}, u32[]{:S(2)}) copy-start(s32[128,2]{0,1:T(2,128)} %param.18) | copy-start | bytes 3076
  6.5 1.9 %copy-start.8 = (s32[4,3]{1,0:T(4,128)S(1)}, s32[4,3]{1,0:T(4,128)}, u32[]{:S(2)}) copy-start(s32[4,3]{1,0:T(4,128)} %param.15) | copy-start | bytes 148
  6.5 2.5 %copy-start.10 = (s32[1,4]{1,0:T(1,128)S(1)}, s32[1,4]{1,0:T(1,128)}, u32[]{:S(2)}) copy-start(s32[1,4]{1,0:T(1,128)} %param.16) | copy-start | bytes 52
  6.5 4.5 %copy-start.3 = (bf16[128,512]{1,0:T(8,128)(2,1)S(1)}, bf16[128,512]{1,0:T(8,128)(2,1)}, u32[]{:S(2)}) copy-start(bf16[128,512]{1,0:T(8,128)(2,1)} %param.12) | copy-start | bytes 393220
  6.5 4.7 %copy-start.4 = (bf16[128,512]{1,0:T(8,128)(2,1)S(1)}, bf16[128,512]{1,0:T(8,128)(2,1)}, u32[]{:S(2)}) copy-start(bf16[128,512]{1,0:T(8,128)(2,1)} %param.13) | copy-start | bytes 393220
  6.5 4.8 %copy-start.5 = (bf16[128,512]{1,0:T(8,128)(2,1)S(1)}, bf16[128,512]{1,0:T(8,128)(2,1)}, u32[]{:S(2)}) copy-start(bf16[128,512]{1,0:T(8,128)(2,1)} %param.14) | copy-start | bytes 393220
  6.6 49.1 %all-gather.5.cloned.1.call-start = ((), (), s32[]{:S(2)}) async-start(), calls=%async_computation.4 | async-start | bytes 6291456 | tf_op jit(solution)/shard_map/all_gather | solution.py:98
  7.3 5.5 %copy-start = (bf16[128,512]{1,0:T(8,128)(2,1)S(1)}, bf16[128,512]{1,0:T(8,128)(2,1)}, u32[]{:S(2)}) copy-start(bf16[128,512]{1,0:T(8,128)(2,1)} %param.11) | copy-start | bytes 393220
  7.3 8.4 %copy-start.7 = (f32[512]{0:T(512)S(1)}, f32[512]{0:T(512)}, u32[]{:S(2)}) copy-start(f32[512]{0:T(512)} %param.17) | copy-start | bytes 6148
  7.3 48.3 %all-gather.7.cloned.1.call-start = ((), (), s32[]{:S(2)}) async-start(), calls=%async_computation.5 | async-start | bytes 6291456 | tf_op jit(solution)/shard_map/all_gather | solution.py:99
  11.0 6.3 %copy-start.1 = (s32[128,2]{1,0:T(8,128)}, s32[128,2]{1,0:T(8,128)S(1)}, u32[]{:S(2)}) copy-start(s32[128,2]{1,0:T(8,128)S(1)} %reshape.208) | copy-start | bytes 3076
  17.3 33.2 %all-to-all-start = ((bf16[8,128,512]{2,1,0:T(8,128)(2,1)}), bf16[8,128,512]{2,1,0:T(8,128)(2,1)S(1)}, u32[]{:S(2)}, u32[]{:S(2)}) async-start(bf16[8,128,512]{2,1,0:T(8,128)(2,1)} %bitcast.12), calls=%async_computation | async-start | bytes 2097152 | tf_op jit(solution)/shard_map/all_to_all | solution.py:94
  64.4 25.2 %copy-start.2 = (s32[128,2]{1,0:T(8,128)S(1)}, s32[128,2]{1,0:T(8,128)}, u32[]{:S(2)}) copy-start(s32[128,2]{1,0:T(8,128)} %copy-done.1) | copy-start | bytes 3076
  64.4 25.4 %copy-start.9 = (s32[128,2]{0,1:T(2,128)S(1)}, s32[128,2]{0,1:T(2,128)}, u32[]{:S(2)}) copy-start(s32[128,2]{0,1:T(2,128)} %param.19) | copy-start | bytes 3076
  70.8 14.2 %collective-permute-start = (bf16[1024,256]{1,0:T(8,128)(2,1)}, bf16[1024,256]{1,0:T(8,128)(2,1)S(1)}, u32[]{:S(2)}, u32[]{:S(2)}) collective-permute-start(bf16[1024,256]{1,0:T(8,128)(2,1)} %dynamic-slice_convert_fusion), channel_id=1, source_target_pairs={{0,2},{2,0},{4,6},{6,4},{8,10},{10,8},{12,14},{14,12},{1,3},{3,1},... | collective-permute-start | bytes 1572872 | tf_op jit(solution)/shard_map/ppermute | solution.py:15
  86.0 17.7 %all-to-all-start.3 = ((bf16[8,128,256]{2,1,0:T(8,128)(2,1)}), bf16[8,128,256]{2,1,0:T(8,128)(2,1)S(1)}, u32[]{:S(2)}, u32[]{:S(2)}) async-start(bf16[8,128,256]{2,1,0:T(8,128)(2,1)} %bitcast.21), calls=%async_computation.3 | async-start | bytes 1048576 | tf_op jit(solution)/shard_map/all_to_all | solution.py:113
Sparse Core Ops, SparseCore 0:
  8.9 16.3 all-gather.4
  26.9 14.8 all-gather.6
where the time goes:
time: 113 us
  waiting for transfers between devices  54.1 us (48%)
  between operations  13.7 us (12%)
  blocking collectives  12.7 us (11%)
  starting transfers between devices  12.3 us (11%)
  matrix products  11.4 us (10%)
  local copies, waits for them, and re-layouts  5.28 us (5%)
  other arithmetic  3.11 us (3%)
    all_to_all x1, waiting for transfers between devices, per_device(): lax.all_to_all(outgoing, 'dev', split_axis=0, concat_axis=0, tiled=True)  26.1 us
    all_to_all x1, waiting for transfers between devices, per_device(): lax.all_to_all(finished, 'dev', split_axis=0, concat_axis=1, tiled=True)  13.8 us
    ppermute x1, waiting for transfers between devices, from_partner(): lax.ppermute(value, axis, [(i, i ^ 1 << bit) for i in range(lax.axis_size...  12.7 us
    dot_general x1, matrix products, per_device(): served_out = jnp.dot(hidden, down_whole, preferred_element_type=jnp.float32)  8.52 us
    all_to_all x1, starting transfers between devices, per_device(): lax.all_to_all(outgoing, 'dev', split_axis=0, concat_axis=0, tiled=True)  7.13 us
    all_to_all x1, blocking collectives, per_device(): lax.all_to_all(served_out, 'tp', split_axis=1, concat_axis=0, tiled=True)  5.55 us
    all_to_all x1, blocking collectives, per_device(): lax.all_to_all(arrived, 'tp', split_axis=0, concat_axis=1, tiled=True)  4.56 us
    all_to_all x1, starting transfers between devices, per_device(): lax.all_to_all(finished, 'dev', split_axis=0, concat_axis=1, tiled=True)  3.65 us
  transfers between devices with their start and end apart: 5, of which 3 were waited for; matrix products, arithmetic and copies ran while one was open for 6% of the time, Pallas kernels for 0%

commit v1 on v0

--- a/solution.py
+++ b/solution.py
@@ -1,6 +1,10 @@
+import functools
+
 import jax
 import jax.numpy as jnp
 from jax import lax
+from jax.experimental import pallas as pl
+from jax.experimental.pallas import tpu as pltpu
 from jax.sharding import PartitionSpec as P
 
 D = 1024
@@ -128,6 +132,341 @@
     return (stream + added).astype(jnp.bfloat16)
 
 
+AUX = 128
+LANES = 128
+
+
+def pair_attention(query_pair, key_pair, value_pair, allowed, low_lanes):
+    nodes = query_pair.shape[0]
+    zero = jnp.zeros_like(query_pair)
+    stacked = jnp.concatenate(
+        [jnp.where(low_lanes, query_pair, zero), jnp.where(low_lanes, zero, query_pair)], axis=0
+    )
+    scores = lax.dot_general(
+        stacked, key_pair, (((1,), (1,)), ((), ())), preferred_element_type=jnp.float32
+    ) * HEAD ** (-0.5)
+    scores = jnp.where(allowed, scores, -1e30)
+    highest = jnp.max(scores, axis=1, keepdims=True)
+    weights = jnp.where(allowed, jnp.exp(scores - highest), 0.0)
+    denominator = jnp.sum(weights, axis=1, keepdims=True)
+    probs = (weights / denominator).astype(jnp.bfloat16)
+    both = jnp.dot(probs, value_pair, preferred_element_type=jnp.float32)
+    return jnp.where(low_lanes, both[:nodes], both[nodes:])
+
+
+def layer_kernel(
+    rows_z,
+    tile_ref,
+    count_ref,
+    residual_ref,
+    query_ref,
+    key_ref,
+    value_ref,
+    gain_ref,
+    ids_ref,
+    codes_ref,
+    up_ref,
+    down_ref,
+    out_ref,
+    gathered,
+    stream,
+    w_up,
+    w_down,
+    hidden,
+    kept,
+    a_out,
+    a_in,
+    b_out,
+    b_in,
+    c_out,
+    c_in,
+    w_sem,
+    send_sem,
+    piece_sem,
+    a_sem,
+    b_sem,
+    c_sem,
+):
+    nodes, half = residual_ref.shape
+    ff = up_ref.shape[2]
+    width = 2 * half
+    dev = lax.axis_index("dev")
+    core = lax.axis_index("tp")
+    z, x = dev // 2, dev % 2
+    other_core = 1 - core
+    other_x = 1 - x
+
+    def z_of(step):
+        flip = 0
+        bit = 1
+        while bit < rows_z:
+            if step & bit:
+                flip = flip + bit * (1 - 2 * ((z // bit) % 2))
+            bit *= 2
+        return z + flip
+
+    load_up = pltpu.make_async_copy(up_ref.at[0], w_up, w_sem.at[0])
+    load_down = pltpu.make_async_copy(down_ref.at[0], w_down, w_sem.at[1])
+    load_up.start()
+    load_down.start()
+
+    barrier = pltpu.get_barrier_semaphore()
+    to_core = {"tp": other_core}
+    to_x = {"dev": 2 * z + other_x}
+    to_z = [{"dev": 2 * z_of(step) + x} for step in range(rows_z)]
+    peers = [to_core, to_x] + to_z[1:]
+    for peer in peers:
+        pl.semaphore_signal(barrier, inc=1, device_id=peer, device_id_type=pl.DeviceIdType.MESH)
+
+    row = lax.broadcasted_iota(jnp.int32, (nodes, nodes), 0)
+    column = lax.broadcasted_iota(jnp.int32, (nodes, nodes), 1)
+    tile_count, listed = tile_ref.shape
+    tile = nodes // tile_count
+    column_tile = column // tile
+    in_list = jnp.zeros((nodes, nodes), jnp.int32)
+    for t in range(tile_count):
+        hit = jnp.zeros((nodes, nodes), jnp.int32)
+        for entry in range(listed):
+            hit = jnp.where(column_tile == tile_ref[t, entry], 1, hit)
+        in_list = jnp.where(row // tile == t, hit, in_list)
+    row_graph = jnp.zeros((nodes, nodes), jnp.int32)
+    column_graph = jnp.zeros((nodes, nodes), jnp.int32)
+    end = 0
+    for g in range(count_ref.shape[1]):
+        end = end + count_ref[0, g]
+        row_graph = row_graph + jnp.where(row >= end, 1, 0)
+        column_graph = column_graph + jnp.where(column >= end, 1, 0)
+    allowed_int = jnp.where((column <= row) & (row_graph == column_graph), in_list, 0)
+    allowed = jnp.concatenate([allowed_int, allowed_int], axis=0) > 0
+    low_lanes = lax.broadcasted_iota(jnp.int32, (nodes, LANES), 1) < HEAD
+
+    own_rows = pl.ds(pl.multiple_of(x * nodes, nodes), nodes)
+    other_rows = pl.ds(pl.multiple_of(other_x * nodes, nodes), nodes)
+
+    squares = jnp.zeros((nodes, LANES), jnp.float32)
+    for pair in range(half // LANES):
+        lanes = slice(pair * LANES, (pair + 1) * LANES)
+        attended = pair_attention(
+            query_ref[:, lanes], key_ref[:, lanes], value_ref[:, lanes], allowed, low_lanes
+        )
+        part = residual_ref[:, lanes].astype(jnp.float32) + attended
+        stream[:, lanes] = part
+        squares = squares + part * part
+        gathered[z, core, own_rows, lanes] = (part * gain_ref[:, lanes]).astype(jnp.bfloat16)
+
+    lane = lax.broadcasted_iota(jnp.int32, (nodes, AUX), 1)
+    total = jnp.sum(squares, axis=1, keepdims=True)
+    item = lane // 2
+    extra = jnp.where(item == rows_z, total, 0.0)
+    for k in range(TOPK):
+        gate = codes_ref[:, k : k + 1].astype(jnp.float32) / 65536.0
+        extra = extra + jnp.where(item == ids_ref[:, k : k + 1], gate, 0.0)
+    coarse = extra.astype(jnp.bfloat16)
+    rest = (extra - coarse.astype(jnp.float32)).astype(jnp.bfloat16)
+    gathered[z, core, own_rows, half:] = jnp.where(lane % 2 == 0, coarse.astype(jnp.float32), rest.astype(jnp.float32)).astype(jnp.bfloat16)
+
+    def remote(src, dst, sent, received, device):
+        return pltpu.make_async_remote_copy(
+            src_ref=src,
+            dst_ref=dst,
+            send_sem=sent,
+            recv_sem=received,
+            device_id=device,
+            device_id_type=pl.DeviceIdType.MESH,
+        )
+
+    def piece(zz, feature_half, xx, kind, step, device):
+        rows = pl.ds(pl.multiple_of(xx * nodes, nodes), nodes)
+        ref = gathered.at[zz, feature_half, rows]
+        return remote(
+            ref, ref, send_sem.at[kind, step], piece_sem.at[zz, feature_half, xx], device
+        )
+
+    started = []
+
+    def start(copy):
+        copy.start()
+        started.append(copy)
+
+    def spread(step):
+        zz = z_of(step)
+        if step:
+            piece(zz, core, x, 0, step, to_z[step]).wait_recv()
+        start(piece(zz, core, x, 1, step, to_x))
+        start(piece(zz, core, x, 2, step, to_core))
+
+    def spread_other(step):
+        zz = z_of(step)
+        piece(zz, core, other_x, 1, step, to_x).wait_recv()
+        start(piece(zz, core, other_x, 3, step, to_core))
+
+    def copy_a(step):
+        return remote(
+            a_out.at[step], a_in.at[step], send_sem.at[4, step], a_sem.at[step], to_core
+        )
+
+    def copy_b(step):
+        return remote(b_out.at[step], b_in.at[step], send_sem.at[5, step], b_sem.at[step], to_x)
+
+    def copy_c(step):
+        return remote(
+            c_out.at[step], c_in.at[step], send_sem.at[6, step], c_sem.at[step], to_z[step]
+        )
+
+    own_lanes = pl.ds(pl.multiple_of(core * half, half), half)
+    other_lanes = pl.ds(pl.multiple_of(other_core * half, half), half)
+
+    def compute(step):
+        zz = z_of(step)
+        piece(zz, other_core, x, 2, step, to_core).wait_recv()
+        piece(zz, other_core, other_x, 3, step, to_core).wait_recv()
+        aux_low = gathered[zz, 0, :, half:].astype(jnp.float32)
+        aux_high = gathered[zz, 1, :, half:].astype(jnp.float32)
+        item = lax.broadcasted_iota(jnp.int32, (2 * nodes, AUX), 1) // 2
+        square = jnp.sum(jnp.where(item == rows_z, aux_low + aux_high, 0.0), axis=1, keepdims=True)
+        scale = lax.rsqrt(square / width + epsilon)
+        gate = jnp.sum(jnp.where(item == z, aux_low, 0.0), axis=1, keepdims=True)
+        chunk = half
+
+        @pl.loop(0, ff // chunk)
+        def _(j):
+            lanes = pl.ds(pl.multiple_of(j * chunk, chunk), chunk)
+            pre = jnp.dot(
+                gathered[zz, 0, :, :half], w_up[:half, lanes], preferred_element_type=jnp.float32
+            ) + jnp.dot(
+                gathered[zz, 1, :, :half], w_up[half:, lanes], preferred_element_type=jnp.float32
+            )
+            hidden[:, lanes] = jax.nn.gelu(pre * scale).astype(jnp.bfloat16)
+
+        sent = jnp.dot(hidden[...], w_down[:, other_lanes], preferred_element_type=jnp.float32)
+        a_out[step] = (sent * gate).astype(jnp.bfloat16)
+        start(copy_a(step))
+        stays = jnp.dot(hidden[...], w_down[:, own_lanes], preferred_element_type=jnp.float32)
+        kept[step] = stays * gate
+
+    def add_cores(step):
+        copy_a(step).wait_recv()
+        b_out[step] = (
+            kept[step, other_rows] + a_in[step, other_rows].astype(jnp.float32)
+        ).astype(jnp.bfloat16)
+        start(copy_b(step))
+
+    def add_columns(step):
+        copy_b(step).wait_recv()
+        total = (
+            kept[step, own_rows]
+            + a_in[step, own_rows].astype(jnp.float32)
+            + b_in[step].astype(jnp.float32)
+        )
+        if step:
+            c_out[step] = total.astype(jnp.bfloat16)
+            start(copy_c(step))
+        else:
+            stream[...] += total
+
+    pl.semaphore_wait(barrier, len(peers))
+    for step in range(1, rows_z):
+        start(piece(z, core, x, 0, step, to_z[step]))
+    spread(0)
+    spread_other(0)
+    load_up.wait()
+    load_down.wait()
+    for step in range(rows_z + 2):
+        if step + 1 < rows_z:
+            spread(step + 1)
+        if 1 <= step <= rows_z:
+            add_cores(step - 1)
+        if step < rows_z:
+            compute(step)
+        if step >= 2:
+            add_columns(step - 2)
+        if step + 1 < rows_z:
+            spread_other(step + 1)
+
+    result = stream[...]
+    for step in range(1, rows_z):
+        copy_c(step).wait_recv()
+        result = result + c_in[step].astype(jnp.float32)
+    out_ref[...] = result.astype(jnp.bfloat16)
+    for copy in started:
+        copy.wait_send()
+
+
+def fused_device(
+    residual,
+    queries,
+    keys,
+    values,
+    tile_lists,
+    node_counts,
+    norm_gain,
+    expert_ids,
+    gate_codes,
+    up_weight,
+    down_weight,
+):
+    nodes, half = residual.shape
+    ff = up_weight.shape[2]
+    rows_z = lax.axis_size("dev") // 2
+    bf16, f32 = jnp.bfloat16, jnp.float32
+    vmem = pl.BlockSpec(memory_space=pltpu.VMEM)
+    smem = pl.BlockSpec(memory_space=pltpu.SMEM)
+    hbm = pl.BlockSpec(memory_space=pl.ANY)
+    return pl.pallas_call(
+        functools.partial(layer_kernel, rows_z),
+        out_shape=jax.ShapeDtypeStruct((nodes, half), bf16),
+        in_specs=[smem, smem] + [vmem] * 7 + [hbm] * 2,
+        out_specs=vmem,
+        scratch_shapes=[
+            pltpu.VMEM((rows_z, 2, 2 * nodes, half + AUX), bf16),
+            pltpu.VMEM((nodes, half), f32),
+            pltpu.VMEM(up_weight.shape[1:], bf16),
+            pltpu.VMEM(down_weight.shape[1:], bf16),
+            pltpu.VMEM((2 * nodes, ff), bf16),
+            pltpu.VMEM((rows_z, 2 * nodes, half), f32),
+            pltpu.VMEM((rows_z, 2 * nodes, half), bf16),
+            pltpu.VMEM((rows_z, 2 * nodes, half), bf16),
+            pltpu.VMEM((rows_z, nodes, half), bf16),
+            pltpu.VMEM((rows_z, nodes, half), bf16),
+            pltpu.VMEM((rows_z, nodes, half), bf16),
+            pltpu.VMEM((rows_z, nodes, half), bf16),
+            pltpu.SemaphoreType.DMA((2,)),
+            pltpu.SemaphoreType.DMA((7, rows_z)),
+            pltpu.SemaphoreType.DMA((rows_z, 2, 2)),
+            pltpu.SemaphoreType.DMA((rows_z,)),
+            pltpu.SemaphoreType.DMA((rows_z,)),
+            pltpu.SemaphoreType.DMA((rows_z,)),
+        ],
+        compiler_params=pltpu.CompilerParams(
+            collective_id=0, has_side_effects=True, vmem_limit_bytes=40 * 1024 * 1024
+        ),
+    )(
+        tile_lists,
+        node_counts,
+        residual,
+        queries,
+        keys,
+        values,
+        norm_gain.reshape(1, half),
+        expert_ids,
+        gate_codes,
+        up_weight,
+        down_weight,
+    )
+
+
+def gathers_all(devices, nodes):
+    experts = devices // 2
+    capacity = 8 * nodes // devices
+    return capacity >= nodes and experts & (experts - 1) == 0 and experts <= 8
+
+
+def layer(residual, *others):
+    if gathers_all(lax.axis_size("dev"), residual.shape[0]):
+        return fused_device(residual, *others)
+    return per_device(residual, *others)
+
+
 def solution(mesh):
     in_specs = (
         P(("groups", "dev"), "tp"),
@@ -144,5 +483,5 @@
     )
     out_specs = P(("groups", "dev"), "tp")
     return jax.shard_map(
-        per_device, mesh=mesh, in_specs=in_specs, out_specs=out_specs, check_vma=False
-    )
+        layer, mesh=mesh, in_specs=in_specs, out_specs=out_specs, check_vma=False
+    )

time: 113 us -> 56.4 us (0.50)
  waiting for transfers between devices: 54.1 us -> 0 us
  Pallas kernels: 0 us -> 45 us
  between operations: 13.7 us -> 0.02 us
  blocking collectives: 12.7 us -> 0 us
  starting transfers between devices: 12.3 us -> 0 us
  matrix products: 11.4 us -> 0 us
  local copies, waits for them, and re-layouts: 5.28 us -> 11 us
  other arithmetic: 3.11 us -> 0 us
    pallas_call x0 -> x1, Pallas kernels: none -> 45 us  [fused_device(): pl.pallas_call(functools.partial(layer_kernel, rows_z), out_shape=jax.Sha...]
    all_to_all x2 -> x0, waiting for transfers between devices: 39.9 us -> none  [the longest x1 26.1 us: per_device(): lax.all_to_all(outgoing, 'dev', split_axis=0, concat_axis=0, tiled=True)]
    ppermute x1 -> x0, waiting for transfers between devices: 12.7 us -> none  [from_partner(): lax.ppermute(value, axis, [(i, i ^ 1 << bit) for i in range(lax.axis_size...]
    dot_general x6 -> x0, matrix products: 11 us -> none  [the longest x1 8.52 us: per_device(): served_out = jnp.dot(hidden, down_whole, preferred_element_type=jnp.float32)]
    all_to_all x2 -> x0, starting transfers between devices: 10.8 us -> none  [the longest x1 7.13 us: per_device(): lax.all_to_all(outgoing, 'dev', split_axis=0, concat_axis=0, tiled=True)]
    unnamed x27 -> x21, local copies, waits for them, and re-layouts: 0.63 us -> 11 us
    all_to_all x2 -> x0, blocking collectives: 10.1 us -> none  [the longest x1 5.55 us: per_device(): lax.all_to_all(served_out, 'tp', split_axis=1, concat_axis=0, tiled=True)]
    psum x1 -> x0, blocking collectives: 2.58 us -> none  [per_device(): squares = lax.psum(jnp.sum(stream * stream, axis=1), 'tp')]
  transfers between devices with their start and end apart: 5 -> 0, of which waited for: 3 -> 0; matrix products, arithmetic and copies ran while one was open for 6% -> 0% of each run, Pallas kernels for 0% -> 0%
where the time goes in v1:
time: 56.4 us; the launch traced here: 56.1 us
  Pallas kernels  45 us (80%)
  local copies, waits for them, and re-layouts  11 us (20%)
    pallas_call x1, Pallas kernels, fused_device(): pl.pallas_call(functools.partial(layer_kernel, rows_z), out_shape=jax.Sha...  45 us
    unnamed x21, local copies, waits for them, and re-layouts  11 us

profile of v1, /device:TPU:0, one launch (start us, length us, event | category | flops | bytes accessed | tf_op | source)
XLA Modules:
  0.0 56.1 jit_solution(17938837145559569273)
XLA Ops:
  0.0 0.8 %copy.12.ids_ref = s32[128,2]{1,0:T(8,128)S(1)} copy(s32[128,2]{0,1:T(2,128)} %param.18) | data formatting | bytes 2048 | tf_op args[7]
  0.8 0.8 %copy.13.codes_ref = s32[128,2]{1,0:T(8,128)S(1)} copy(s32[128,2]{0,1:T(2,128)} %param.19) | data formatting | bytes 2048 | tf_op args[8]
  1.6 0.0 copy-start
  1.6 1.6 %copy-done = bf16[1,1024,1024]{2,1,0:T(8,128)(2,1)S(1)} copy-done((bf16[1,1024,1024]{2,1,0:T(8,128)(2,1)S(1)}, bf16[1,1024,1024]{2,1,0:T(8,128)(2,1)}, u32[]{:S(2)}) %copy-start) | copy-done | bytes 2097176
  3.2 0.0 copy-start.1
  3.2 1.6 %copy-done.1 = bf16[1,1024,1024]{2,1,0:T(8,128)(2,1)S(1)} copy-done((bf16[1,1024,1024]{2,1,0:T(8,128)(2,1)S(1)}, bf16[1,1024,1024]{2,1,0:T(8,128)(2,1)}, u32[]{:S(2)}) %copy-start.1) | copy-done | bytes 2097176
  4.8 0.0 copy-start.2
  4.8 0.9 %copy-done.2 = bf16[128,512]{1,0:T(8,128)(2,1)S(1)} copy-done((bf16[128,512]{1,0:T(8,128)(2,1)S(1)}, bf16[128,512]{1,0:T(8,128)(2,1)}, u32[]{:S(2)}) %copy-start.2) | copy-done | bytes 131096
  5.7 0.0 copy-start.3
  5.7 0.9 %copy-done.3 = bf16[128,512]{1,0:T(8,128)(2,1)S(1)} copy-done((bf16[128,512]{1,0:T(8,128)(2,1)S(1)}, bf16[128,512]{1,0:T(8,128)(2,1)}, u32[]{:S(2)}) %copy-start.3) | copy-done | bytes 131096
  6.6 0.0 copy-start.4
  6.6 0.9 %copy-done.4 = bf16[128,512]{1,0:T(8,128)(2,1)S(1)} copy-done((bf16[128,512]{1,0:T(8,128)(2,1)S(1)}, bf16[128,512]{1,0:T(8,128)(2,1)}, u32[]{:S(2)}) %copy-start.4) | copy-done | bytes 131096
  7.5 0.0 copy-start.5
  7.5 0.9 %copy-done.5 = bf16[128,512]{1,0:T(8,128)(2,1)S(1)} copy-done((bf16[128,512]{1,0:T(8,128)(2,1)S(1)}, bf16[128,512]{1,0:T(8,128)(2,1)}, u32[]{:S(2)}) %copy-start.5) | copy-done | bytes 131096
  8.4 0.0 copy-start.6
  8.4 0.7 %copy-done.6 = s32[4,3]{1,0:T(4,128)S(1)} copy-done((s32[4,3]{1,0:T(4,128)S(1)}, s32[4,3]{1,0:T(4,128)}, u32[]{:S(2)}) %copy-start.6) | copy-done | bytes 72
  9.1 0.0 copy-start.7
  9.1 0.7 %copy-done.7 = f32[512]{0:T(512)S(1)} copy-done((f32[512]{0:T(512)S(1)}, f32[512]{0:T(512)}, u32[]{:S(2)}) %copy-start.7) | copy-done | bytes 2072
  9.7 0.0 copy-start.8
  9.7 0.7 %copy-done.8 = s32[1,4]{1,0:T(1,128)S(1)} copy-done((s32[1,4]{1,0:T(1,128)S(1)}, s32[1,4]{1,0:T(1,128)}, u32[]{:S(2)}) %copy-start.8) | copy-done | bytes 40
  10.4 45.0 %shard_map.109 = bf16[128,512]{1,0:T(8,128)(2,1)S(1)} custom-call(s32[4,3]{1,0:T(4,128)S(1)} %copy-done.6, s32[1,4]{1,0:T(1,128)S(1)} %copy-done.8, bf16[128,512]{1,0:T(8,128)(2,1)S(1)} %copy-done.2, bf16[128,512]{1,0:T(8,128)(2,1)S(1)} %copy-done.3, bf16[128,512]{1,0:T(8,128)(2,1)S(1)} %copy-done.4, bf16[128,512]{1,0:T(8,128)(2,1)S(1)} %copy-done.5, ...), custom_call_target="tpu_custom_call" | custom-call | tf_op jit(solution)/shard_map/pallas_call | solution.py:415
  55.4 0.7 %copy.15 = bf16[128,512]{1,0:T(8,128)(2,1)} copy(bf16[128,512]{1,0:T(8,128)(2,1)S(1)} %shard_map.109) | data formatting | bytes 262144
Async XLA Ops:
  1.6 1.6 %copy-start = (bf16[1,1024,1024]{2,1,0:T(8,128)(2,1)S(1)}, bf16[1,1024,1024]{2,1,0:T(8,128)(2,1)}, u32[]{:S(2)}) copy-start(bf16[1,1024,1024]{2,1,0:T(8,128)(2,1)} %up_ref.1) | copy-start | bytes 6291460
  3.2 1.6 %copy-start.1 = (bf16[1,1024,1024]{2,1,0:T(8,128)(2,1)S(1)}, bf16[1,1024,1024]{2,1,0:T(8,128)(2,1)}, u32[]{:S(2)}) copy-start(bf16[1,1024,1024]{2,1,0:T(8,128)(2,1)} %down_ref.1) | copy-start | bytes 6291460
  4.8 0.9 %copy-start.2 = (bf16[128,512]{1,0:T(8,128)(2,1)S(1)}, bf16[128,512]{1,0:T(8,128)(2,1)}, u32[]{:S(2)}) copy-start(bf16[128,512]{1,0:T(8,128)(2,1)} %residual_ref.1) | copy-start | bytes 393220
  5.7 0.9 %copy-start.3 = (bf16[128,512]{1,0:T(8,128)(2,1)S(1)}, bf16[128,512]{1,0:T(8,128)(2,1)}, u32[]{:S(2)}) copy-start(bf16[128,512]{1,0:T(8,128)(2,1)} %query_ref.1) | copy-start | bytes 393220
  6.6 0.9 %copy-start.4 = (bf16[128,512]{1,0:T(8,128)(2,1)S(1)}, bf16[128,512]{1,0:T(8,128)(2,1)}, u32[]{:S(2)}) copy-start(bf16[128,512]{1,0:T(8,128)(2,1)} %key_ref.1) | copy-start | bytes 393220
  7.5 0.9 %copy-start.5 = (bf16[128,512]{1,0:T(8,128)(2,1)S(1)}, bf16[128,512]{1,0:T(8,128)(2,1)}, u32[]{:S(2)}) copy-start(bf16[128,512]{1,0:T(8,128)(2,1)} %value_ref.1) | copy-start | bytes 393220
  8.4 0.7 %copy-start.6 = (s32[4,3]{1,0:T(4,128)S(1)}, s32[4,3]{1,0:T(4,128)}, u32[]{:S(2)}) copy-start(s32[4,3]{1,0:T(4,128)} %tile_ref.1) | copy-start | bytes 148
  9.1 0.7 %copy-start.7 = (f32[512]{0:T(512)S(1)}, f32[512]{0:T(512)}, u32[]{:S(2)}) copy-start(f32[512]{0:T(512)} %param.17) | copy-start | bytes 6148
  9.7 0.7 %copy-start.8 = (s32[1,4]{1,0:T(1,128)S(1)}, s32[1,4]{1,0:T(1,128)}, u32[]{:S(2)}) copy-start(s32[1,4]{1,0:T(1,128)} %count_ref.1) | copy-start | bytes 52

commit v2 on v1

--- a/solution.py
+++ b/solution.py
@@ -132,7 +132,7 @@
     return (stream + added).astype(jnp.bfloat16)
 
 
-AUX = 128
+AUX = 16
 LANES = 128
 
 
@@ -156,6 +156,18 @@
 
 def layer_kernel(
     rows_z,
+    tile_hbm,
+    count_hbm,
+    residual_hbm,
+    query_hbm,
+    key_hbm,
+    value_hbm,
+    gain_hbm,
+    ids_hbm,
+    codes_hbm,
+    up_ref,
+    down_ref,
+    out_ref,
     tile_ref,
     count_ref,
     residual_ref,
@@ -165,9 +177,6 @@
     gain_ref,
     ids_ref,
     codes_ref,
-    up_ref,
-    down_ref,
-    out_ref,
     gathered,
     stream,
     w_up,
@@ -205,6 +214,21 @@
             bit *= 2
         return z + flip
 
+    small = []
+    for hbm, near in (
+        (tile_hbm, tile_ref),
+        (count_hbm, count_ref),
+        (query_hbm, query_ref),
+        (key_hbm, key_ref),
+        (value_hbm, value_ref),
+        (residual_hbm, residual_ref),
+        (gain_hbm, gain_ref),
+        (ids_hbm, ids_ref),
+        (codes_hbm, codes_ref),
+    ):
+        copy = pltpu.make_async_copy(hbm, near, w_sem.at[2 + len(small)])
+        copy.start()
+        small.append(copy)
     load_up = pltpu.make_async_copy(up_ref.at[0], w_up, w_sem.at[0])
     load_down = pltpu.make_async_copy(down_ref.at[0], w_down, w_sem.at[1])
     load_up.start()
@@ -217,6 +241,9 @@
     peers = [to_core, to_x] + to_z[1:]
     for peer in peers:
         pl.semaphore_signal(barrier, inc=1, device_id=peer, device_id_type=pl.DeviceIdType.MESH)
+
+    for copy in small:
+        copy.wait()
 
     row = lax.broadcasted_iota(jnp.int32, (nodes, nodes), 0)
     column = lax.broadcasted_iota(jnp.int32, (nodes, nodes), 1)
@@ -252,18 +279,20 @@
         part = residual_ref[:, lanes].astype(jnp.float32) + attended
         stream[:, lanes] = part
         squares = squares + part * part
-        gathered[z, core, own_rows, lanes] = (part * gain_ref[:, lanes]).astype(jnp.bfloat16)
-
-    lane = lax.broadcasted_iota(jnp.int32, (nodes, AUX), 1)
-    total = jnp.sum(squares, axis=1, keepdims=True)
-    item = lane // 2
-    extra = jnp.where(item == rows_z, total, 0.0)
+        gathered[z, core, x, :nodes, lanes] = (part * gain_ref[:, lanes]).astype(jnp.bfloat16)
+
+    item = lax.broadcasted_iota(jnp.int32, (AUX, nodes), 0)
+    total = jnp.sum(squares.T, axis=0, keepdims=True)
+    extra = jnp.where(item // 2 == rows_z, total, 0.0)
     for k in range(TOPK):
-        gate = codes_ref[:, k : k + 1].astype(jnp.float32) / 65536.0
-        extra = extra + jnp.where(item == ids_ref[:, k : k + 1], gate, 0.0)
-    coarse = extra.astype(jnp.bfloat16)
-    rest = (extra - coarse.astype(jnp.float32)).astype(jnp.bfloat16)
-    gathered[z, core, own_rows, half:] = jnp.where(lane % 2 == 0, coarse.astype(jnp.float32), rest.astype(jnp.float32)).astype(jnp.bfloat16)
+        gate = codes_ref[k : k + 1, :].astype(jnp.float32) / 65536.0
+        extra = extra + jnp.where(item // 2 == ids_ref[k : k + 1, :], gate, 0.0)
+    coarse = extra.astype(jnp.bfloat16).astype(jnp.float32)
+    extra = jnp.where(item % 2 == 0, coarse, extra - coarse).astype(jnp.bfloat16)
+    gathered[z, core, x, nodes:, :LANES] = extra
+    for pair in range(1, half // LANES):
+        lanes = slice(pair * LANES, (pair + 1) * LANES)
+        gathered[z, core, x, nodes:, lanes] = jnp.zeros((AUX, LANES), jnp.bfloat16)
 
     def remote(src, dst, sent, received, device):
         return pltpu.make_async_remote_copy(
@@ -276,8 +305,7 @@
         )
 
     def piece(zz, feature_half, xx, kind, step, device):
-        rows = pl.ds(pl.multiple_of(xx * nodes, nodes), nodes)
-        ref = gathered.at[zz, feature_half, rows]
+        ref = gathered.at[zz, feature_half, xx]
         return remote(
             ref, ref, send_sem.at[kind, step], piece_sem.at[zz, feature_half, xx], device
         )
@@ -320,21 +348,41 @@
         zz = z_of(step)
         piece(zz, other_core, x, 2, step, to_core).wait_recv()
         piece(zz, other_core, other_x, 3, step, to_core).wait_recv()
-        aux_low = gathered[zz, 0, :, half:].astype(jnp.float32)
-        aux_high = gathered[zz, 1, :, half:].astype(jnp.float32)
-        item = lax.broadcasted_iota(jnp.int32, (2 * nodes, AUX), 1) // 2
-        square = jnp.sum(jnp.where(item == rows_z, aux_low + aux_high, 0.0), axis=1, keepdims=True)
+        item = lax.broadcasted_iota(jnp.int32, (AUX, LANES), 0) // 2
+        pick_square = jnp.where(item == rows_z, 1.0, 0.0).astype(jnp.bfloat16)
+        pick_gate = jnp.where(item == z, 1.0, 0.0).astype(jnp.bfloat16)
+
+        def column_of(feature_half, pick):
+            return jnp.concatenate(
+                [
+                    lax.dot_general(
+                        gathered[zz, feature_half, xx, nodes:, :LANES],
+                        pick,
+                        (((0,), (0,)), ((), ())),
+                        preferred_element_type=jnp.float32,
+                    )[:, :1]
+                    for xx in range(2)
+                ],
+                axis=0,
+            )
+
+        def rows_of(feature_half):
+            return jnp.concatenate(
+                [gathered[zz, feature_half, xx, :nodes] for xx in range(2)], axis=0
+            )
+
+        square = column_of(0, pick_square) + column_of(1, pick_square)
         scale = lax.rsqrt(square / width + epsilon)
-        gate = jnp.sum(jnp.where(item == z, aux_low, 0.0), axis=1, keepdims=True)
+        gate = column_of(0, pick_gate)
         chunk = half
 
         @pl.loop(0, ff // chunk)
         def _(j):
             lanes = pl.ds(pl.multiple_of(j * chunk, chunk), chunk)
             pre = jnp.dot(
-                gathered[zz, 0, :, :half], w_up[:half, lanes], preferred_element_type=jnp.float32
+                rows_of(0), w_up[:half, lanes], preferred_element_type=jnp.float32
             ) + jnp.dot(
-                gathered[zz, 1, :, :half], w_up[half:, lanes], preferred_element_type=jnp.float32
+                rows_of(1), w_up[half:, lanes], preferred_element_type=jnp.float32
             )
             hidden[:, lanes] = jax.nn.gelu(pre * scale).astype(jnp.bfloat16)
 
@@ -409,16 +457,23 @@
     ff = up_weight.shape[2]
     rows_z = lax.axis_size("dev") // 2
     bf16, f32 = jnp.bfloat16, jnp.float32
-    vmem = pl.BlockSpec(memory_space=pltpu.VMEM)
-    smem = pl.BlockSpec(memory_space=pltpu.SMEM)
     hbm = pl.BlockSpec(memory_space=pl.ANY)
     return pl.pallas_call(
         functools.partial(layer_kernel, rows_z),
         out_shape=jax.ShapeDtypeStruct((nodes, half), bf16),
-        in_specs=[smem, smem] + [vmem] * 7 + [hbm] * 2,
-        out_specs=vmem,
+        in_specs=[hbm] * 11,
+        out_specs=pl.BlockSpec(memory_space=pltpu.VMEM),
         scratch_shapes=[
-            pltpu.VMEM((rows_z, 2, 2 * nodes, half + AUX), bf16),
+            pltpu.SMEM(tile_lists.shape, jnp.int32),
+            pltpu.SMEM(node_counts.shape, jnp.int32),
+            pltpu.VMEM((nodes, half), bf16),
+            pltpu.VMEM((nodes, half), bf16),
+            pltpu.VMEM((nodes, half), bf16),
+            pltpu.VMEM((nodes, half), bf16),
+            pltpu.VMEM((1, half), f32),
+            pltpu.VMEM((TOPK, nodes), jnp.int32),
+            pltpu.VMEM((TOPK, nodes), jnp.int32),
+            pltpu.VMEM((rows_z, 2, 2, nodes + AUX, half), bf16),
             pltpu.VMEM((nodes, half), f32),
             pltpu.VMEM(up_weight.shape[1:], bf16),
             pltpu.VMEM(down_weight.shape[1:], bf16),
@@ -430,7 +485,7 @@
             pltpu.VMEM((rows_z, nodes, half), bf16),
             pltpu.VMEM((rows_z, nodes, half), bf16),
             pltpu.VMEM((rows_z, nodes, half), bf16),
-            pltpu.SemaphoreType.DMA((2,)),
+            pltpu.SemaphoreType.DMA((11,)),
             pltpu.SemaphoreType.DMA((7, rows_z)),
             pltpu.SemaphoreType.DMA((rows_z, 2, 2)),
             pltpu.SemaphoreType.DMA((rows_z,)),
@@ -438,7 +493,7 @@
             pltpu.SemaphoreType.DMA((rows_z,)),
         ],
         compiler_params=pltpu.CompilerParams(
-            collective_id=0, has_side_effects=True, vmem_limit_bytes=40 * 1024 * 1024
+            collective_id=0, has_side_effects=True, vmem_limit_bytes=63 * 1024 * 1024
         ),
     )(
         tile_lists,
@@ -448,8 +503,8 @@
         keys,
         values,
         norm_gain.reshape(1, half),
-        expert_ids,
-        gate_codes,
+        expert_ids.T,
+        gate_codes.T,
         up_weight,
         down_weight,
     )
@@ -458,7 +513,7 @@
 def gathers_all(devices, nodes):
     experts = devices // 2
     capacity = 8 * nodes // devices
-    return capacity >= nodes and experts & (experts - 1) == 0 and experts <= 8
+    return capacity >= nodes and experts & (experts - 1) == 0 and experts < 8
 
 
 def layer(residual, *others):

time: 56.4 us -> 46.9 us (0.83)
  local copies, waits for them, and re-layouts: 11 us -> 1.57 us
    unnamed x21 -> x1, local copies, waits for them, and re-layouts: 11 us -> 1.57 us
where the time goes in v2:
time: 46.9 us; the launch traced here: 46.8 us
  Pallas kernels  45.2 us (96%)
  local copies, waits for them, and re-layouts  1.57 us (3%)
    pallas_call x1, Pallas kernels, fused_device(): pl.pallas_call(functools.partial(layer_kernel, rows_z), out_shape=jax.Sha...  45.2 us
    unnamed x1, local copies, waits for them, and re-layouts  1.57 us

profile of v2, /device:TPU:0, one launch (start us, length us, event | category | flops | bytes accessed | tf_op | source)
XLA Modules:
  0.0 46.8 jit_solution(9429658138096548695)
XLA Ops:
  0.0 45.2 %shard_map.109 = bf16[128,512]{1,0:T(8,128)(2,1)} custom-call(s32[4,3]{1,0:T(4,128)} %tile_hbm.1, s32[1,4]{1,0:T(1,128)} %count_hbm.1, bf16[128,512]{1,0:T(8,128)(2,1)} %residual_hbm.1, bf16[128,512]{1,0:T(8,128)(2,1)} %query_hbm.1, bf16[128,512]{1,0:T(8,128)(2,1)} %key_hbm.1, bf16[128,512]{1,0:T(8,128)(2,1)} %value_hbm.1, f32[1,512]{1,0:T(1,128)} %bitcast.3, ...), custom_call_target="tpu_custom_call" | custom-call | tf_op jit(solution)/shard_map/pallas_call | solution.py:461
  45.2 1.6 %copy.13 = bf16[128,512]{1,0:T(8,128)(2,1)} copy(bf16[128,512]{1,0:T(8,128)(2,1)} %shard_map.109) | data formatting | bytes 262144

commit v3 on v2

--- a/solution.py
+++ b/solution.py
@@ -133,6 +133,7 @@
 
 
 AUX = 16
+CHUNKS = 2
 LANES = 128
 
 
@@ -205,14 +206,20 @@
     other_core = 1 - core
     other_x = 1 - x
 
+    orders = []
+    for place in range(rows_z):
+        order = [place]
+        for distance in range(1, rows_z):
+            order += [r for r in (place + distance, place - distance) if 0 <= r < rows_z]
+        orders.append(order)
+
     def z_of(step):
-        flip = 0
-        bit = 1
-        while bit < rows_z:
-            if step & bit:
-                flip = flip + bit * (1 - 2 * ((z // bit) % 2))
-            bit *= 2
-        return z + flip
+        found = orders[0][step]
+        for place in range(1, rows_z):
+            found = jnp.where(z == place, orders[place][step], found)
+        return found
+
+    z_order = [z] + [z_of(step) for step in range(1, rows_z)]
 
     small = []
     for hbm, near in (
@@ -237,7 +244,8 @@
     barrier = pltpu.get_barrier_semaphore()
     to_core = {"tp": other_core}
     to_x = {"dev": 2 * z + other_x}
-    to_z = [{"dev": 2 * z_of(step) + x} for step in range(rows_z)]
+    to_z = [{"dev": 2 * zz + x} for zz in z_order]
+    to_above, to_below = {"dev": dev + 2}, {"dev": dev - 2}
     peers = [to_core, to_x] + to_z[1:]
     for peer in peers:
         pl.semaphore_signal(barrier, inc=1, device_id=peer, device_id_type=pl.DeviceIdType.MESH)
@@ -271,6 +279,7 @@
     other_rows = pl.ds(pl.multiple_of(other_x * nodes, nodes), nodes)
 
     squares = jnp.zeros((nodes, LANES), jnp.float32)
+    piece_lanes = half // CHUNKS
     for pair in range(half // LANES):
         lanes = slice(pair * LANES, (pair + 1) * LANES)
         attended = pair_attention(
@@ -279,7 +288,10 @@
         part = residual_ref[:, lanes].astype(jnp.float32) + attended
         stream[:, lanes] = part
         squares = squares + part * part
-        gathered[z, core, x, :nodes, lanes] = (part * gain_ref[:, lanes]).astype(jnp.bfloat16)
+        chunk, offset = pair * LANES // piece_lanes, pair * LANES % piece_lanes
+        gathered[z, core, x, chunk, :nodes, offset : offset + LANES] = (
+            part * gain_ref[:, lanes]
+        ).astype(jnp.bfloat16)
 
     item = lax.broadcasted_iota(jnp.int32, (AUX, nodes), 0)
     total = jnp.sum(squares.T, axis=0, keepdims=True)
@@ -289,10 +301,8 @@
         extra = extra + jnp.where(item // 2 == ids_ref[k : k + 1, :], gate, 0.0)
     coarse = extra.astype(jnp.bfloat16).astype(jnp.float32)
     extra = jnp.where(item % 2 == 0, coarse, extra - coarse).astype(jnp.bfloat16)
-    gathered[z, core, x, nodes:, :LANES] = extra
-    for pair in range(1, half // LANES):
-        lanes = slice(pair * LANES, (pair + 1) * LANES)
-        gathered[z, core, x, nodes:, lanes] = jnp.zeros((AUX, LANES), jnp.bfloat16)
+    gathered[z, core, x, 0, nodes:, :LANES] = extra
+    gathered[z, core, x, 0, nodes:, LANES:] = jnp.zeros((AUX, piece_lanes - LANES), jnp.bfloat16)
 
     def remote(src, dst, sent, received, device):
         return pltpu.make_async_remote_copy(
@@ -304,50 +314,78 @@
             device_id_type=pl.DeviceIdType.MESH,
         )
 
-    def piece(zz, feature_half, xx, kind, step, device):
-        ref = gathered.at[zz, feature_half, xx]
+    def piece(zz, feature_half, xx, kind, step, chunk, device):
+        ref = gathered.at[zz, feature_half, xx, chunk, pl.ds(0, nodes if chunk else nodes + AUX)]
         return remote(
-            ref, ref, send_sem.at[kind, step], piece_sem.at[zz, feature_half, xx], device
+            ref,
+            ref,
+            send_sem.at[kind, step, chunk],
+            piece_sem.at[zz, feature_half, xx, chunk],
+            device,
         )
 
     started = []
 
-    def start(copy):
-        copy.start()
-        started.append(copy)
-
-    def spread(step):
-        zz = z_of(step)
+    def start(copy, condition=None):
+        if condition is None:
+            copy.start()
+        else:
+            pl.when(condition)(lambda: copy.start())
+        started.append((copy, condition))
+
+    def spread(step, chunk):
+        zz = z_order[step]
         if step:
-            piece(zz, core, x, 0, step, to_z[step]).wait_recv()
-        start(piece(zz, core, x, 1, step, to_x))
-        start(piece(zz, core, x, 2, step, to_core))
-
-    def spread_other(step):
-        zz = z_of(step)
-        piece(zz, core, other_x, 1, step, to_x).wait_recv()
-        start(piece(zz, core, other_x, 3, step, to_core))
+            piece(zz, core, x, 0, step, chunk, to_z[step]).wait_recv()
+            start(piece(zz, core, x, 0, step, chunk, to_below), (zz > z) & (z > 0))
+            start(piece(zz, core, x, 7, step, chunk, to_above), (zz < z) & (z < rows_z - 1))
+        else:
+            start(piece(zz, core, x, 0, 0, chunk, to_below), z > 0)
+            start(piece(zz, core, x, 7, 0, chunk, to_above), z < rows_z - 1)
+        start(piece(zz, core, x, 1, step, chunk, to_x))
+        start(piece(zz, core, x, 2, step, chunk, to_core))
+
+    def spread_other(step, chunk):
+        zz = z_order[step]
+        piece(zz, core, other_x, 1, step, chunk, to_x).wait_recv()
+        start(piece(zz, core, other_x, 3, step, chunk, to_core))
 
     def copy_a(step):
         return remote(
-            a_out.at[step], a_in.at[step], send_sem.at[4, step], a_sem.at[step], to_core
+            a_out.at[step], a_in.at[step], send_sem.at[4, step, 0], a_sem.at[step], to_core
         )
 
-    def copy_b(step):
-        return remote(b_out.at[step], b_in.at[step], send_sem.at[5, step], b_sem.at[step], to_x)
-
-    def copy_c(step):
+    def half_rows(part):
+        return pl.ds(part * (nodes // 2), nodes // 2)
+
+    def copy_b(step, part):
+        rows = half_rows(part)
         return remote(
-            c_out.at[step], c_in.at[step], send_sem.at[6, step], c_sem.at[step], to_z[step]
+            b_out.at[step, rows],
+            b_in.at[step, rows],
+            send_sem.at[5, step, part],
+            b_sem.at[step, part],
+            to_x,
+        )
+
+    def copy_c(step, part, source):
+        rows = half_rows(part)
+        return remote(
+            c_out.at[step, rows],
+            c_in.at[source, rows],
+            send_sem.at[6, step, part],
+            c_sem.at[source, part],
+            to_z[step],
         )
 
     own_lanes = pl.ds(pl.multiple_of(core * half, half), half)
     other_lanes = pl.ds(pl.multiple_of(other_core * half, half), half)
 
-    def compute(step):
-        zz = z_of(step)
-        piece(zz, other_core, x, 2, step, to_core).wait_recv()
-        piece(zz, other_core, other_x, 3, step, to_core).wait_recv()
+    def compute(step, between):
+        zz = z_order[step]
+        for chunk in range(CHUNKS):
+            piece(zz, other_core, x, 2, step, chunk, to_core).wait_recv()
+            piece(zz, other_core, other_x, 3, step, chunk, to_core).wait_recv()
         item = lax.broadcasted_iota(jnp.int32, (AUX, LANES), 0) // 2
         pick_square = jnp.where(item == rows_z, 1.0, 0.0).astype(jnp.bfloat16)
         pick_gate = jnp.where(item == z, 1.0, 0.0).astype(jnp.bfloat16)
@@ -356,7 +394,7 @@
             return jnp.concatenate(
                 [
                     lax.dot_general(
-                        gathered[zz, feature_half, xx, nodes:, :LANES],
+                        gathered[zz, feature_half, xx, 0, nodes:, :LANES],
                         pick,
                         (((0,), (0,)), ((), ())),
                         preferred_element_type=jnp.float32,
@@ -368,7 +406,14 @@
 
         def rows_of(feature_half):
             return jnp.concatenate(
-                [gathered[zz, feature_half, xx, :nodes] for xx in range(2)], axis=0
+                [
+                    jnp.concatenate(
+                        [gathered[zz, feature_half, xx, chunk, :nodes] for chunk in range(CHUNKS)],
+                        axis=1,
+                    )
+                    for xx in range(2)
+                ],
+                axis=0,
             )
 
         square = column_of(0, pick_square) + column_of(1, pick_square)
@@ -386,6 +431,7 @@
             )
             hidden[:, lanes] = jax.nn.gelu(pre * scale).astype(jnp.bfloat16)
 
+        between()
         sent = jnp.dot(hidden[...], w_down[:, other_lanes], preferred_element_type=jnp.float32)
         a_out[step] = (sent * gate).astype(jnp.bfloat16)
         start(copy_a(step))
@@ -397,47 +443,67 @@
         b_out[step] = (
             kept[step, other_rows] + a_in[step, other_rows].astype(jnp.float32)
         ).astype(jnp.bfloat16)
-        start(copy_b(step))
+        for part in range(2):
+            start(copy_b(step, part))
 
     def add_columns(step):
-        copy_b(step).wait_recv()
-        total = (
-            kept[step, own_rows]
-            + a_in[step, own_rows].astype(jnp.float32)
-            + b_in[step].astype(jnp.float32)
-        )
-        if step:
-            c_out[step] = total.astype(jnp.bfloat16)
-            start(copy_c(step))
-        else:
-            stream[...] += total
+        for part in range(2):
+            copy_b(step, part).wait_recv()
+            first = pl.multiple_of(x * nodes + part * (nodes // 2), nodes // 2)
+            rows = pl.ds(first, nodes // 2)
+            total = (
+                kept[step, rows]
+                + a_in[step, rows].astype(jnp.float32)
+                + b_in[step, half_rows(part)].astype(jnp.float32)
+            )
+            if step:
+                c_out[step, half_rows(part)] = total.astype(jnp.bfloat16)
+                start(copy_c(step, part, z))
+            else:
+                stream[half_rows(part)] += total
 
     pl.semaphore_wait(barrier, len(peers))
-    for step in range(1, rows_z):
-        start(piece(z, core, x, 0, step, to_z[step]))
-    spread(0)
-    spread_other(0)
+    for chunk in range(CHUNKS):
+        spread(0, chunk)
+    for chunk in range(CHUNKS):
+        spread(1, chunk)
+        spread_other(0, chunk)
     load_up.wait()
     load_down.wait()
-    for step in range(rows_z + 2):
+    for step in range(rows_z):
+
+        def between(step=step):
+            if step + 2 < rows_z:
+                spread(step + 2, 0)
+            if step == rows_z - 1:
+                add_columns(step - 2)
+
+        compute(step, between)
+        if step + 2 < rows_z:
+            for chunk in range(1, CHUNKS):
+                spread(step + 2, chunk)
         if step + 1 < rows_z:
-            spread(step + 1)
-        if 1 <= step <= rows_z:
-            add_cores(step - 1)
-        if step < rows_z:
-            compute(step)
-        if step >= 2:
-            add_columns(step - 2)
-        if step + 1 < rows_z:
-            spread_other(step + 1)
+            for chunk in range(CHUNKS):
+                spread_other(step + 1, chunk)
+        if step >= 1:
+            add_cores(step)
+    add_columns(2)
+    add_columns(3)
+    add_cores(0)
+    add_columns(0)
 
     result = stream[...]
     for step in range(1, rows_z):
-        copy_c(step).wait_recv()
-        result = result + c_in[step].astype(jnp.float32)
+        zz = z_order[step]
+        for part in range(2):
+            copy_c(step, part, zz).wait_recv()
+        result = result + c_in[zz].astype(jnp.float32)
     out_ref[...] = result.astype(jnp.bfloat16)
-    for copy in started:
-        copy.wait_send()
+    for copy, condition in started:
+        if condition is None:
+            copy.wait_send()
+        else:
+            pl.when(condition)(lambda copy=copy: copy.wait_send())
 
 
 def fused_device(
@@ -473,7 +539,7 @@
             pltpu.VMEM((1, half), f32),
             pltpu.VMEM((TOPK, nodes), jnp.int32),
             pltpu.VMEM((TOPK, nodes), jnp.int32),
-            pltpu.VMEM((rows_z, 2, 2, nodes + AUX, half), bf16),
+            pltpu.VMEM((rows_z, 2, 2, CHUNKS, nodes + AUX, half // CHUNKS), bf16),
             pltpu.VMEM((nodes, half), f32),
             pltpu.VMEM(up_weight.shape[1:], bf16),
             pltpu.VMEM(down_weight.shape[1:], bf16),
@@ -486,11 +552,11 @@
             pltpu.VMEM((rows_z, nodes, half), bf16),
             pltpu.VMEM((rows_z, nodes, half), bf16),
             pltpu.SemaphoreType.DMA((11,)),
-            pltpu.SemaphoreType.DMA((7, rows_z)),
-            pltpu.SemaphoreType.DMA((rows_z, 2, 2)),
+            pltpu.SemaphoreType.DMA((8, rows_z, CHUNKS)),
+            pltpu.SemaphoreType.DMA((rows_z, 2, 2, CHUNKS)),
             pltpu.SemaphoreType.DMA((rows_z,)),
-            pltpu.SemaphoreType.DMA((rows_z,)),
-            pltpu.SemaphoreType.DMA((rows_z,)),
+            pltpu.SemaphoreType.DMA((rows_z, 2)),
+            pltpu.SemaphoreType.DMA((rows_z, 2)),
         ],
         compiler_params=pltpu.CompilerParams(
             collective_id=0, has_side_effects=True, vmem_limit_bytes=63 * 1024 * 1024
@@ -513,7 +579,7 @@
 def gathers_all(devices, nodes):
     experts = devices // 2
     capacity = 8 * nodes // devices
-    return capacity >= nodes and experts & (experts - 1) == 0 and experts < 8
+    return capacity >= nodes and 4 <= experts < 8
 
 
 def layer(residual, *others):

time: 46.9 us -> 44.1 us (0.940)
  Pallas kernels: 45.2 us -> 42.3 us
    pallas_call x1, Pallas kernels: 45.2 us -> 42.3 us  [fused_device(): pl.pallas_call(functools.partial(layer_kernel, rows_z), out_shape=jax.Sha...]
where the time goes in v3:
time: 44.1 us; the launch traced here: 43.9 us
  Pallas kernels  42.3 us (96%)
  local copies, waits for them, and re-layouts  1.57 us (4%)
    pallas_call x1, Pallas kernels, fused_device(): pl.pallas_call(functools.partial(layer_kernel, rows_z), out_shape=jax.Sha...  42.3 us
    unnamed x1, local copies, waits for them, and re-layouts  1.57 us

profile of v3, /device:TPU:0, one launch (start us, length us, event | category | flops | bytes accessed | tf_op | source)
XLA Modules:
  0.0 43.9 jit_solution(12357535899957390130)
XLA Ops:
  0.0 42.3 %shard_map.109 = bf16[128,512]{1,0:T(8,128)(2,1)} custom-call(s32[4,3]{1,0:T(4,128)} %tile_hbm.1, s32[1,4]{1,0:T(1,128)} %count_hbm.1, bf16[128,512]{1,0:T(8,128)(2,1)} %residual_hbm.1, bf16[128,512]{1,0:T(8,128)(2,1)} %query_hbm.1, bf16[128,512]{1,0:T(8,128)(2,1)} %key_hbm.1, bf16[128,512]{1,0:T(8,128)(2,1)} %value_hbm.1, f32[1,512]{1,0:T(1,128)} %bitcast.3, ...), custom_call_target="tpu_custom_call" | custom-call | tf_op jit(solution)/shard_map/pallas_call | solution.py:527
  42.3 1.6 %copy.13 = bf16[128,512]{1,0:T(8,128)(2,1)} copy(bf16[128,512]{1,0:T(8,128)(2,1)} %shard_map.109) | data formatting | bytes 262144

commit v4 on v3

--- a/solution.py
+++ b/solution.py
@@ -350,9 +350,14 @@
         piece(zz, core, other_x, 1, step, chunk, to_x).wait_recv()
         start(piece(zz, core, other_x, 3, step, chunk, to_core))
 
-    def copy_a(step):
+    def copy_a(step, part):
+        rows = own_rows if part else other_rows
         return remote(
-            a_out.at[step], a_in.at[step], send_sem.at[4, step, 0], a_sem.at[step], to_core
+            a_out.at[step, rows],
+            a_in.at[step, rows],
+            send_sem.at[4, step, part],
+            a_sem.at[step, part],
+            to_core,
         )
 
     def half_rows(part):
@@ -434,19 +439,23 @@
         between()
         sent = jnp.dot(hidden[...], w_down[:, other_lanes], preferred_element_type=jnp.float32)
         a_out[step] = (sent * gate).astype(jnp.bfloat16)
-        start(copy_a(step))
+        for part in range(2):
+            start(copy_a(step, part))
         stays = jnp.dot(hidden[...], w_down[:, own_lanes], preferred_element_type=jnp.float32)
         kept[step] = stays * gate
 
     def add_cores(step):
-        copy_a(step).wait_recv()
-        b_out[step] = (
-            kept[step, other_rows] + a_in[step, other_rows].astype(jnp.float32)
-        ).astype(jnp.bfloat16)
+        copy_a(step, 0).wait_recv()
         for part in range(2):
+            first = pl.multiple_of(other_x * nodes + part * (nodes // 2), nodes // 2)
+            rows = pl.ds(first, nodes // 2)
+            b_out[step, half_rows(part)] = (
+                kept[step, rows] + a_in[step, rows].astype(jnp.float32)
+            ).astype(jnp.bfloat16)
             start(copy_b(step, part))
 
     def add_columns(step):
+        copy_a(step, 1).wait_recv()
         for part in range(2):
             copy_b(step, part).wait_recv()
             first = pl.multiple_of(x * nodes + part * (nodes // 2), nodes // 2)
@@ -554,7 +563,7 @@
             pltpu.SemaphoreType.DMA((11,)),
             pltpu.SemaphoreType.DMA((8, rows_z, CHUNKS)),
             pltpu.SemaphoreType.DMA((rows_z, 2, 2, CHUNKS)),
-            pltpu.SemaphoreType.DMA((rows_z,)),
+            pltpu.SemaphoreType.DMA((rows_z, 2)),
             pltpu.SemaphoreType.DMA((rows_z, 2)),
             pltpu.SemaphoreType.DMA((rows_z, 2)),
         ],

time: 44.1 us -> 43.9 us (level)
  no operation moved by 1% of the time
where the time goes in v4:
time: 43.9 us; the launch traced here: 43.7 us
  Pallas kernels  42.2 us (96%)
  local copies, waits for them, and re-layouts  1.57 us (4%)
    pallas_call x1, Pallas kernels, fused_device(): pl.pallas_call(functools.partial(layer_kernel, rows_z), out_shape=jax.Sha...  42.2 us
    unnamed x1, local copies, waits for them, and re-layouts  1.57 us

profile of v4, /device:TPU:0, one launch (start us, length us, event | category | flops | bytes accessed | tf_op | source)
XLA Modules:
  0.0 43.7 jit_solution(17329063547924895185)
XLA Ops:
  0.0 42.2 %shard_map.109 = bf16[128,512]{1,0:T(8,128)(2,1)} custom-call(s32[4,3]{1,0:T(4,128)} %tile_hbm.1, s32[1,4]{1,0:T(1,128)} %count_hbm.1, bf16[128,512]{1,0:T(8,128)(2,1)} %residual_hbm.1, bf16[128,512]{1,0:T(8,128)(2,1)} %query_hbm.1, bf16[128,512]{1,0:T(8,128)(2,1)} %key_hbm.1, bf16[128,512]{1,0:T(8,128)(2,1)} %value_hbm.1, f32[1,512]{1,0:T(1,128)} %bitcast.3, ...), custom_call_target="tpu_custom_call" | custom-call | tf_op jit(solution)/shard_map/pallas_call | solution.py:536
  42.2 1.6 %copy.13 = bf16[128,512]{1,0:T(8,128)(2,1)} copy(bf16[128,512]{1,0:T(8,128)(2,1)} %shard_map.109) | data formatting | bytes 262144
